TPU v7x, 32 devices: a whole 2x2x4 slice. The times are simulated.
32 devices in a mesh: tile: 4 (over y, x), head: 8 (over z, core).
Axes of the slice: x: 2, y: 2, z: 4, core: 2. Of those that a mesh axis runs over, the one named last changes fastest.
Arguments:
- embedded: bfloat16 [4, 1024, 16, 16], P('tile', 'head'), may hold values from -6 to 6
- cotangent: bfloat16 [4, 1024, 16, 16], P('tile', 'head'), may hold values from -6 to 6
- weights: bfloat16 [1024, 4, 8, 128], P('head'), may hold values from -0.1875 to 0.1875
Outputs:
- attention: bfloat16 [4, 1024, 16, 16], P('tile', 'head')
- token_grads: float32 [4, 1024, 16, 16], P('tile', 'head')
- weight_grads: float32 [1024, 4, 8, 128], P('head')
All inputs are finite; a program needn't handle non-finite values.
Results may differ from a plain program's by a relative error of at most 0.022.
Values may be sent and summed in bfloat16 or wider, within the bound.
A program may use at most 64 MiB of HBM per device.

v0:
```python
import jax
import jax.numpy as jnp
from jax import lax
from jax.sharding import PartitionSpec as P

D = 1024
HEADS = 8
HEAD_DIM = 128
TILE_ROWS = 16
TILE_COLS = 16
RIM = 4
PAD_ROWS = 24
PAD_COLS = 24
TILE_TOKENS = 256
PAD_TOKENS = 576


def passed_along(value, axis, steps):
    count = lax.axis_size(axis)
    leading, last = (max(0, -steps), min(count, count - steps))
    return lax.ppermute(value, axis, [(source, source + steps) for source in range(leading, last)])


def contract(first_op, second_op, first_dim, second_dim):
    return lax.dot_general(
        first_op,
        second_op,
        (((first_dim,), (second_dim,)), ((), ())),
        preferred_element_type=jnp.float32,
    )


def rim_move(piece, shift_by):
    return passed_along(piece.astype(jnp.bfloat16), "tile", shift_by).astype(piece.dtype)


def spread_units(units, per_dev, short_devs):
    if short_devs == 0:
        return units
    head_count = short_devs * (per_dev - 1)
    lead = units[:head_count].reshape((short_devs, per_dev - 1) + units.shape[1:])
    filler = jnp.zeros((short_devs, 1) + units.shape[1:], units.dtype)
    lead = jnp.concatenate([lead, filler], 1).reshape((short_devs * per_dev,) + units.shape[1:])
    return jnp.concatenate([lead, units[head_count:]], 0)


def pack_units(whole, per_dev, short_devs):
    if short_devs == 0:
        return whole
    lead = whole[: short_devs * per_dev].reshape((short_devs, per_dev) + whole.shape[1:])
    lead = lead[:, : per_dev - 1].reshape((short_devs * (per_dev - 1),) + whole.shape[1:])
    return jnp.concatenate([lead, whole[short_devs * per_dev :]], 0)


def local(embedded, cotangent, weights):
    score_scale = HEAD_DIM ** (-0.5)
    n_head = lax.axis_size("head")
    n_tile = lax.axis_size("tile")
    tile_group = n_head // HEADS
    strip_cols = embedded.shape[3]
    width_part = embedded.shape[1]
    tile_id = lax.axis_index("tile")
    head_id = lax.axis_index("head")
    parity = tile_id % 2
    tile_slot = head_id // HEADS
    own_block = embedded[0].astype(jnp.float32)
    from_left = rim_move(own_block[:, :, strip_cols - RIM :], 1)
    from_right = rim_move(own_block[:, :, :RIM], -1)
    from_left = jnp.where(parity == 1, from_left, 0.0)
    from_right = jnp.where(parity == 0, from_right, 0.0)
    widened = jnp.concatenate([from_left, own_block, from_right], 2)
    from_above = rim_move(widened[:, TILE_ROWS - RIM :, :], 2)
    from_below = rim_move(widened[:, :RIM, :], -2)
    padded = jnp.concatenate([from_above, widened, from_below], 1).astype(jnp.bfloat16)
    tile_stack = jnp.stack(
        [
            padded[:, :, member * TILE_COLS : member * TILE_COLS + PAD_COLS]
            for member in range(tile_group)
        ]
    )
    token_send = jnp.repeat(tile_stack.reshape(tile_group, width_part, PAD_TOKENS), HEADS, axis=0)
    grad_tiles = (
        cotangent[0].reshape(width_part, TILE_ROWS, tile_group, TILE_COLS).transpose(2, 0, 1, 3)
    )
    grad_send = jnp.repeat(grad_tiles.reshape(tile_group, width_part, TILE_TOKENS), HEADS, axis=0)
    weight_send = jnp.tile(
        weights.transpose(2, 0, 1, 3).reshape(HEADS, width_part, 4 * HEAD_DIM), (tile_group, 1, 1)
    )
    tokens_in, grads_in, weights_in = (
        lax.all_to_all(token_send, "head", split_axis=0, concat_axis=1, tiled=True),
        lax.all_to_all(grad_send, "head", split_axis=0, concat_axis=1, tiled=True),
        lax.all_to_all(weight_send, "head", split_axis=0, concat_axis=1, tiled=True),
    )
    tokens_all = tokens_in[0]
    grads_all = grads_in[0]
    weight_head = weights_in[0]
    row_pos = tile_id // 2 * TILE_ROWS + jnp.arange(PAD_ROWS) - RIM
    col_pos = (parity * tile_group + tile_slot) * TILE_COLS + jnp.arange(PAD_COLS) - RIM
    height = n_tile // 2 * TILE_ROWS
    breadth = 2 * tile_group * TILE_COLS
    key_valid = (
        ((row_pos >= 0) & (row_pos < height))[:, None]
        & ((col_pos >= 0) & (col_pos < breadth))[None, :]
    ).reshape(PAD_TOKENS)
    interior = tokens_all.reshape(D, PAD_ROWS, PAD_COLS)[
        :, RIM : RIM + TILE_ROWS, RIM : RIM + TILE_COLS
    ].reshape(D, TILE_TOKENS)
    w_query = weight_head[:, :HEAD_DIM]
    w_keyval = weight_head[:, HEAD_DIM : 3 * HEAD_DIM]
    w_out = weight_head[:, 3 * HEAD_DIM :]
    queries = contract(interior, w_query, 0, 0).astype(jnp.bfloat16)
    keyval = contract(tokens_all, w_keyval, 0, 0).astype(jnp.bfloat16)
    keys = keyval[:, :HEAD_DIM]
    values = keyval[:, HEAD_DIM:]
    scores = contract(queries, keys, 1, 1) * score_scale
    scores = jnp.where(key_valid[None, :], scores, -jnp.inf)
    top_score = jnp.max(scores, axis=-1, keepdims=True)
    expo = jnp.exp(scores - top_score)
    probs = expo / jnp.sum(expo, axis=-1, keepdims=True)
    probs_low = probs.astype(jnp.bfloat16)
    attended = jnp.dot(probs_low, values, preferred_element_type=jnp.float32).astype(jnp.bfloat16)
    partial_value = contract(w_out, attended, 1, 1).astype(jnp.bfloat16)
    part_send = partial_value.reshape(n_head, width_part, TILE_TOKENS)
    d_attended = contract(grads_all, w_out, 0, 0).astype(jnp.bfloat16)
    grad_out_w = contract(grads_all, attended, 1, 0)
    d_probs = contract(d_attended, values, 1, 1)
    d_scores = (
        probs * (d_probs - jnp.sum(d_probs * probs, axis=-1, keepdims=True)) * score_scale
    ).astype(jnp.bfloat16)
    d_queries = jnp.dot(d_scores, keys, preferred_element_type=jnp.float32).astype(jnp.bfloat16)
    d_keys = contract(d_scores, queries, 0, 0).astype(jnp.bfloat16)
    d_values = contract(probs_low, d_attended, 0, 0).astype(jnp.bfloat16)
    d_keyval = jnp.concatenate([d_keys, d_values], 1)
    grad_query_w = jnp.dot(interior, d_queries, preferred_element_type=jnp.float32)
    grad_keyval_w = jnp.dot(tokens_all, d_keyval, preferred_element_type=jnp.float32)
    d_tokens = contract(w_keyval, d_keyval, 1, 1)
    d_inner = contract(w_query, d_queries, 1, 1)
    d_tokens = (
        d_tokens.reshape(D, PAD_ROWS, PAD_COLS)
        .at[:, RIM : RIM + TILE_ROWS, RIM : RIM + TILE_COLS]
        .add(d_inner.reshape(D, TILE_ROWS, TILE_COLS))
    )
    d_tokens = d_tokens.reshape(D, PAD_TOKENS).astype(jnp.bfloat16)
    weight_term = jnp.concatenate([grad_query_w, grad_keyval_w, grad_out_w], 1)
    unit_count = 4 * width_part
    unit_dev = (unit_count + n_tile - 1) // n_tile
    short_devs = unit_dev * n_tile - unit_count
    by_unit = weight_term.reshape(n_head, unit_count, HEAD_DIM).transpose(1, 0, 2)
    spread = spread_units(by_unit, unit_dev, short_devs)
    share = lax.psum_scatter(spread.astype(jnp.bfloat16), "tile", scatter_dimension=0, tiled=True)
    weight_send_back = share.transpose(1, 0, 2)
    grad_send_back = d_tokens.reshape(n_head, width_part, PAD_TOKENS)
    parts_back, grads_back, weights_back = (
        lax.all_to_all(part_send, "head", split_axis=0, concat_axis=0, tiled=True),
        lax.all_to_all(grad_send_back, "head", split_axis=0, concat_axis=0, tiled=True),
        lax.all_to_all(weight_send_back, "head", split_axis=0, concat_axis=0, tiled=True),
    )
    out_sum = jnp.sum(
        parts_back.reshape(tile_group, HEADS, width_part, TILE_TOKENS).astype(jnp.float32), axis=1
    ).astype(jnp.bfloat16)
    attention = (
        out_sum.reshape(tile_group, width_part, TILE_ROWS, TILE_COLS)
        .transpose(1, 2, 0, 3)
        .reshape(1, width_part, TILE_ROWS, strip_cols)
    )
    window_grads = jnp.sum(
        grads_back.reshape(tile_group, HEADS, width_part, PAD_TOKENS).astype(jnp.float32), axis=1
    )
    window_grads = window_grads.reshape(tile_group, width_part, PAD_ROWS, PAD_COLS)
    grad_field = jnp.zeros((width_part, PAD_ROWS, strip_cols + 2 * RIM), jnp.float32)
    for member in range(tile_group):
        grad_field = grad_field.at[:, :, member * TILE_COLS : member * TILE_COLS + PAD_COLS].add(
            window_grads[member]
        )
    to_above = rim_move(grad_field[:, :RIM, :], -2)
    to_below = rim_move(grad_field[:, RIM + TILE_ROWS :, :], 2)
    grad_core = grad_field[:, RIM : RIM + TILE_ROWS, :]
    grad_core = grad_core.at[:, TILE_ROWS - RIM :, :].add(to_above).at[:, :RIM, :].add(to_below)
    back_left = rim_move(grad_core[:, :, :RIM], -1)
    back_right = rim_move(grad_core[:, :, RIM + strip_cols :], 1)
    grad_inner = grad_core[:, :, RIM : RIM + strip_cols]
    grad_inner = grad_inner.at[:, :, strip_cols - RIM :].add(jnp.where(parity == 0, back_left, 0.0))
    grad_inner = grad_inner.at[:, :, :RIM].add(jnp.where(parity == 1, back_right, 0.0))
    token_grads = grad_inner[None]
    slot_sum = jnp.sum(
        weights_back.reshape(tile_group, HEADS, unit_dev, HEAD_DIM).astype(jnp.float32), axis=0
    )
    collected = lax.all_gather(slot_sum.transpose(1, 0, 2), "tile", axis=0, tiled=True)
    weight_grads = pack_units(collected, unit_dev, short_devs).reshape(
        width_part, 4, HEADS, HEAD_DIM
    )
    return (attention, token_grads, weight_grads)


def solution(mesh):
    placed = (
        P("tile", "head", None, None),
        P("tile", "head", None, None),
        P("head", None, None, None),
    )
    return jax.shard_map(
        local,
        mesh=mesh,
        in_specs=placed,
        out_specs=(
            P("tile", "head", None, None),
            P("tile", "head", None, None),
            P("head", None, None, None),
        ),
        check_vma=False,
    )
```

profile of v0, /device:TPU:0, one launch (start us, length us, event | category | flops | bytes accessed | tf_op | source)
XLA Modules:
  0.0 214.3 jit_solution(9662375512927455358)
XLA Ops:
  7.2 1.0 copy.29
  8.2 0.8 reshape.288
  9.0 6.3 %all-to-all-start.3 = ((bf16[8,128,256]{2,1,0:T(8,128)(2,1)}), bf16[8,128,256]{2,1,0:T(8,128)(2,1)S(1)}, u32[]{:S(2)}, u32[]{:S(2)}) async-start(bf16[8,128,256]{2,1,0:T(8,128)(2,1)} %reshape.288), calls=%async_computation.3 | async-start | bytes 1048576 | tf_op jit(solution)/shard_map/all_to_all | solution.py:91
  15.4 1.7 copy.25
  17.1 13.6 %all-to-all-done.3 = bf16[8,128,256]{2,1,0:T(8,128)(2,1)S(1)} async-done(((bf16[8,128,256]{2,1,0:T(8,128)(2,1)}), bf16[8,128,256]{2,1,0:T(8,128)(2,1)S(1)}, u32[]{:S(2)}, u32[]{:S(2)}) %all-to-all-start.3) | async-done | bytes 524320 | tf_op jit(solution)/shard_map/all_to_all | solution.py:91
  30.7 3.6 %all-to-all-start.1 = ((bf16[8,128,512]{1,2,0:T(8,128)(2,1)}), bf16[8,128,512]{1,2,0:T(8,128)(2,1)S(1)}, u32[]{:S(2)}, u32[]{:S(2)}) async-start(bf16[8,128,512]{1,2,0:T(8,128)(2,1)} %bitcast.4), calls=%async_computation.1 | async-start | bytes 2097152 | tf_op jit(solution)/shard_map/all_to_all | solution.py:92
  34.3 3.4 %collective-permute-start = (bf16[128,16,4]{0,2,1:T(4,128)(2,1)S(1)}, bf16[128,16,4]{0,2,1:T(4,128)(2,1)S(1)}, u32[]{:S(2)}, u32[]{:S(2)}) collective-permute-start(bf16[128,16,4]{0,2,1:T(4,128)(2,1)S(1)} %get-tuple-element.101), channel_id=1, source_target_pairs={{0,8},{8,16},{16,24},{1,9},{9,17},{17,25},{2,10},{10,18},{18,26},{... | collective-permute-start | bytes 49160 | tf_op jit(solution)/shard_map/ppermute | solution.py:21
  37.8 1.3 collective-permute-start.1
  39.2 4.2 %collective-permute-done.1 = bf16[128,16,4]{0,2,1:T(4,128)(2,1)S(1)} collective-permute-done((bf16[128,16,4]{0,2,1:T(4,128)(2,1)S(1)}, bf16[128,16,4]{0,2,1:T(4,128)(2,1)S(1)}, u32[]{:S(2)}, u32[]{:S(2)}) %collective-permute-start.1) | collective-permute-done | bytes 16416 | tf_op jit(solution)/shard_map/ppermute | solution.py:21
  43.5 3.4 %collective-permute-start.2 = (bf16[128,4,24]{0,2,1:T(8,128)(2,1)S(1)}, bf16[128,4,24]{0,2,1:T(8,128)(2,1)S(1)}, u32[]{:S(2)}, u32[]{:S(2)}) collective-permute-start(bf16[128,4,24]{0,2,1:T(8,128)(2,1)S(1)} %get-tuple-element.99), channel_id=1, source_target_pairs={{0,16},{8,24},{1,17},{9,25},{2,18},{10,26},{3,19},{11,27},{4,20},{... | collective-permute-start | bytes 73736 | tf_op jit(solution)/shard_map/ppermute | solution.py:21
  46.9 1.3 collective-permute-start.3
  48.2 0.2 collective-permute-done.2
  48.4 4.2 %collective-permute-done.3 = bf16[128,4,24]{0,2,1:T(8,128)(2,1)S(1)} collective-permute-done((bf16[128,4,24]{0,2,1:T(8,128)(2,1)S(1)}, bf16[128,4,24]{0,2,1:T(8,128)(2,1)S(1)}, u32[]{:S(2)}, u32[]{:S(2)}) %collective-permute-start.3) | collective-permute-done | bytes 24608 | tf_op jit(solution)/shard_map/ppermute | solution.py:21
  52.7 8.1 %all-to-all-done.1 = bf16[8,128,512]{1,2,0:T(8,128)(2,1)S(1)} async-done(((bf16[8,128,512]{1,2,0:T(8,128)(2,1)}), bf16[8,128,512]{1,2,0:T(8,128)(2,1)S(1)}, u32[]{:S(2)}, u32[]{:S(2)}) %all-to-all-start.1) | async-done | bytes 1048608 | tf_op jit(solution)/shard_map/all_to_all | solution.py:92
  60.8 1.2 reshape.285
  62.0 3.6 %all-to-all-start = ((bf16[8,128,576]{1,2,0:T(8,128)(2,1)}), bf16[8,128,576]{1,2,0:T(8,128)(2,1)S(1)}, u32[]{:S(2)}, u32[]{:S(2)}) async-start(bf16[8,128,576]{1,2,0:T(8,128)(2,1)} %reshape.285), calls=%async_computation | async-start | bytes 2359296 | tf_op jit(solution)/shard_map/all_to_all | solution.py:90
  65.8 0.5 copy.26
  66.4 1.8 convolution_convert_fusion.8
  68.1 26.7 %all-to-all-done = bf16[8,128,576]{1,2,0:T(8,128)(2,1)S(1)} async-done(((bf16[8,128,576]{1,2,0:T(8,128)(2,1)}), bf16[8,128,576]{1,2,0:T(8,128)(2,1)S(1)}, u32[]{:S(2)}, u32[]{:S(2)}) %all-to-all-start) | async-done | bytes 1179680 | tf_op jit(solution)/shard_map/all_to_all | solution.py:90
  94.9 0.8 copy.24
  95.6 1.4 reshape_squeeze.3
  97.0 1.3 slice.226
  98.4 0.3 convolution_convert_fusion.10
  98.6 0.5 convolution_convert_fusion.2
  99.1 0.3 fusion.37
  99.4 0.1 fusion.8
  99.5 0.3 convolution_convert_fusion.9
  99.9 0.2 convolution_convert_fusion.5
  100.1 0.3 multiply_reduce_fusion
  100.4 0.2 multiply_convert_fusion
  100.6 0.3 convolution_convert_fusion.7
  100.9 0.2 convolution_convert_fusion.6
  101.2 0.3 copy-done.2
  101.5 0.3 fusion.4
  101.8 0.3 convolution_convert_fusion.4
  102.1 0.6 convolution_convert_fusion
  102.8 0.5 copy.31
  103.3 1.4 convert_element_type.118
  104.8 1.4 fusion.9
  106.2 25.3 %reduce-scatter.2.cloned.1.call-done = bf16[128,8,128]{2,0,1:T(8,128)(2,1)} async-done(((bf16[512,8,128]{2,0,1:T(8,128)(2,1)}), bf16[128,8,128]{2,0,1:T(8,128)(2,1)}) %reduce-scatter.2.cloned.1.call-update) | async-done | bytes 262160 | tf_op jit(solution)/shard_map/reduce_scatter | solution.py:150
  131.6 4.6 %all-to-all-start.5 = ((bf16[8,128,128]{2,1,0:T(8,128)(2,1)}), bf16[8,128,128]{2,1,0:T(8,128)(2,1)}, u32[]{:S(2)}, u32[]{:S(2)}) async-start(bf16[8,128,128]{2,1,0:T(8,128)(2,1)} %bitcast.92), calls=%async_computation.6 | async-start | bytes 524288 | tf_op jit(solution)/shard_map/all_to_all | solution.py:156
  136.2 1.1 fusion.14
  137.3 0.3 slice_add_fusion
  137.6 1.3 scatter-add.16
  138.9 0.2 convert_element_type.111
  139.1 0.3 copy.35
  139.4 1.2 copy.30
  140.6 5.4 %all-to-all-done.5 = bf16[8,128,128]{2,1,0:T(8,128)(2,1)} async-done(((bf16[8,128,128]{2,1,0:T(8,128)(2,1)}), bf16[8,128,128]{2,1,0:T(8,128)(2,1)}, u32[]{:S(2)}, u32[]{:S(2)}) %all-to-all-start.5) | async-done | bytes 262176 | tf_op jit(solution)/shard_map/all_to_all | solution.py:156
  146.0 3.6 %all-to-all-start.4 = ((bf16[8,128,576]{1,2,0:T(8,128)(2,1)}), bf16[8,128,576]{1,2,0:T(8,128)(2,1)S(1)}, u32[]{:S(2)}, u32[]{:S(2)}) async-start(bf16[8,128,576]{1,2,0:T(8,128)(2,1)} %copy.30), calls=%async_computation.4 | async-start | bytes 2359296 | tf_op jit(solution)/shard_map/all_to_all | solution.py:155
  149.7 1.8 convert_bitcast_fusion
  151.5 1.2 fusion.1
  152.7 0.9 copy.45
  153.6 25.3 %all-to-all-done.4 = bf16[8,128,576]{1,2,0:T(8,128)(2,1)S(1)} async-done(((bf16[8,128,576]{1,2,0:T(8,128)(2,1)}), bf16[8,128,576]{1,2,0:T(8,128)(2,1)S(1)}, u32[]{:S(2)}, u32[]{:S(2)}) %all-to-all-start.4) | async-done | bytes 1179680 | tf_op jit(solution)/shard_map/all_to_all | solution.py:155
  178.9 3.5 %all-to-all-start.2 = ((bf16[8,128,256]{1,2,0:T(8,128)(2,1)}), bf16[8,128,256]{1,2,0:T(8,128)(2,1)S(1)}, u32[]{:S(2)}, u32[]{:S(2)}) async-start(bf16[8,128,256]{1,2,0:T(8,128)(2,1)} %bitcast.69), calls=%async_computation.2 | async-start | bytes 1048576 | tf_op jit(solution)/shard_map/all_to_all | solution.py:154
  182.4 0.2 convert_reduce_fusion
  182.6 1.3 collective-permute-start.4
  184.0 4.5 %collective-permute-start.5 = (bf16[128,4,24]{0,2,1:T(8,128)(2,1)S(1)}, bf16[128,4,24]{0,2,1:T(8,128)(2,1)S(1)}, u32[]{:S(2)}, u32[]{:S(2)}) collective-permute-start(bf16[128,4,24]{0,2,1:T(8,128)(2,1)S(1)} %get-tuple-element.95), channel_id=1, source_target_pairs={{0,16},{8,24},{1,17},{9,25},{2,18},{10,26},{3,19},{11,27},{4,20},{... | collective-permute-start | bytes 73736 | tf_op jit(solution)/shard_map/ppermute | solution.py:21
  188.5 1.5 collective-permute-done.5
  190.1 1.3 collective-permute-start.6
  191.4 6.3 %all-to-all-done.2 = bf16[8,128,256]{1,2,0:T(8,128)(2,1)S(1)} async-done(((bf16[8,128,256]{1,2,0:T(8,128)(2,1)}), bf16[8,128,256]{1,2,0:T(8,128)(2,1)S(1)}, u32[]{:S(2)}, u32[]{:S(2)}) %all-to-all-start.2) | async-done | bytes 524320 | tf_op jit(solution)/shard_map/all_to_all | solution.py:154
  197.7 0.7 reduce_sum.44
  198.4 3.3 %collective-permute-start.7 = (bf16[128,16,4]{0,2,1:T(4,128)(2,1)S(1)}, bf16[128,16,4]{0,2,1:T(4,128)(2,1)S(1)}, u32[]{:S(2)}, u32[]{:S(2)}) collective-permute-start(bf16[128,16,4]{0,2,1:T(4,128)(2,1)S(1)} %get-tuple-element.97), channel_id=1, source_target_pairs={{0,8},{8,16},{16,24},{1,9},{9,17},{17,25},{2,10},{10,18},{18,26},{... | collective-permute-start | bytes 49160 | tf_op jit(solution)/shard_map/ppermute | solution.py:21
  201.8 1.4 collective-permute-done.7
  203.3 4.2 %copy.32 = f32[128,4,8,128]{3,2,1,0:T(8,128)} copy(f32[128,4,8,128]{3,1,0,2:T(4,128)} %bitcast.85) | data formatting | bytes 4194304
  (48 shorter events, 0.8 us)
Async XLA Ops:
  7.2 8.2 %copy-start.3 = (bf16[128,4,8,128]{3,2,1,0:T(8,128)(2,1)S(1)}, bf16[128,4,8,128]{3,2,1,0:T(8,128)(2,1)}, u32[]{:S(2)}) copy-start(bf16[128,4,8,128]{3,2,1,0:T(8,128)(2,1)} %param.19) | copy-start | bytes 3145732
  9.0 21.7 %all-to-all-start.3 = ((bf16[8,128,256]{2,1,0:T(8,128)(2,1)}), bf16[8,128,256]{2,1,0:T(8,128)(2,1)S(1)}, u32[]{:S(2)}, u32[]{:S(2)}) async-start(bf16[8,128,256]{2,1,0:T(8,128)(2,1)} %reshape.288), calls=%async_computation.3 | async-start | bytes 1048576 | tf_op jit(solution)/shard_map/all_to_all | solution.py:91
  17.1 17.2 %copy-start.8 = (bf16[1,128,16,16]{1,3,2,0:T(8,128)(2,1)S(1)}, bf16[1,128,16,16]{1,3,2,0:T(8,128)(2,1)}, u32[]{:S(2)}) copy-start(bf16[1,128,16,16]{1,3,2,0:T(8,128)(2,1)} %param.17) | copy-start | bytes 196612
  30.7 31.3 %copy-start.1 = (bf16[8,128,256]{2,1,0:T(8,128)(2,1)}, bf16[8,128,256]{2,1,0:T(8,128)(2,1)S(1)}, u32[]{:S(2)}) copy-start(bf16[8,128,256]{2,1,0:T(8,128)(2,1)S(1)} %all-to-all-done.3) | copy-start | bytes 1572868
  30.7 30.1 %all-to-all-start.1 = ((bf16[8,128,512]{1,2,0:T(8,128)(2,1)}), bf16[8,128,512]{1,2,0:T(8,128)(2,1)S(1)}, u32[]{:S(2)}, u32[]{:S(2)}) async-start(bf16[8,128,512]{1,2,0:T(8,128)(2,1)} %bitcast.4), calls=%async_computation.1 | async-start | bytes 2097152 | tf_op jit(solution)/shard_map/all_to_all | solution.py:92
  34.3 4.9 %collective-permute-start = (bf16[128,16,4]{0,2,1:T(4,128)(2,1)S(1)}, bf16[128,16,4]{0,2,1:T(4,128)(2,1)S(1)}, u32[]{:S(2)}, u32[]{:S(2)}) collective-permute-start(bf16[128,16,4]{0,2,1:T(4,128)(2,1)S(1)} %get-tuple-element.101), channel_id=1, source_target_pairs={{0,8},{8,16},{16,24},{1,9},{9,17},{17,25},{2,10},{10,18},{18,26},{... | collective-permute-start | bytes 49160 | tf_op jit(solution)/shard_map/ppermute | solution.py:21
  37.8 5.6 %collective-permute-start.1 = (bf16[128,16,4]{0,2,1:T(4,128)(2,1)S(1)}, bf16[128,16,4]{0,2,1:T(4,128)(2,1)S(1)}, u32[]{:S(2)}, u32[]{:S(2)}) collective-permute-start(bf16[128,16,4]{0,2,1:T(4,128)(2,1)S(1)} %get-tuple-element.102), channel_id=1, source_target_pairs={{8,0},{16,8},{24,16},{9,1},{17,9},{25,17},{10,2},{18,10},{26,18},{... | collective-permute-start | bytes 49160 | tf_op jit(solution)/shard_map/ppermute | solution.py:21
  43.5 4.9 %collective-permute-start.2 = (bf16[128,4,24]{0,2,1:T(8,128)(2,1)S(1)}, bf16[128,4,24]{0,2,1:T(8,128)(2,1)S(1)}, u32[]{:S(2)}, u32[]{:S(2)}) collective-permute-start(bf16[128,4,24]{0,2,1:T(8,128)(2,1)S(1)} %get-tuple-element.99), channel_id=1, source_target_pairs={{0,16},{8,24},{1,17},{9,25},{2,18},{10,26},{3,19},{11,27},{4,20},{... | collective-permute-start | bytes 73736 | tf_op jit(solution)/shard_map/ppermute | solution.py:21
  46.9 5.7 %collective-permute-start.3 = (bf16[128,4,24]{0,2,1:T(8,128)(2,1)S(1)}, bf16[128,4,24]{0,2,1:T(8,128)(2,1)S(1)}, u32[]{:S(2)}, u32[]{:S(2)}) collective-permute-start(bf16[128,4,24]{0,2,1:T(8,128)(2,1)S(1)} %get-tuple-element.100), channel_id=1, source_target_pairs={{16,0},{24,8},{17,1},{25,9},{18,2},{26,10},{19,3},{27,11},{20,4},{... | collective-permute-start | bytes 73736 | tf_op jit(solution)/shard_map/ppermute | solution.py:21
  62.0 32.9 %all-to-all-start = ((bf16[8,128,576]{1,2,0:T(8,128)(2,1)}), bf16[8,128,576]{1,2,0:T(8,128)(2,1)S(1)}, u32[]{:S(2)}, u32[]{:S(2)}) async-start(bf16[8,128,576]{1,2,0:T(8,128)(2,1)} %reshape.285), calls=%async_computation | async-start | bytes 2359296 | tf_op jit(solution)/shard_map/all_to_all | solution.py:90
  65.6 66.0 %reduce-scatter.2.cloned.1.call-start = ((), (), s32[]{:S(2)}) async-start(), calls=%async_computation.7 | async-start | bytes 1310720 | tf_op jit(solution)/shard_map/reduce_scatter | solution.py:150
  66.4 69.8 %copy-start = (bf16[8,128,512]{2,1,0:T(8,128)(2,1)}, bf16[8,128,512]{2,1,0:T(8,128)(2,1)S(1)}, u32[]{:S(2)}) copy-start(bf16[8,128,512]{2,1,0:T(8,128)(2,1)S(1)} %copy.26) | copy-start | bytes 3145732
  99.9 1.3 copy-start.5
  100.1 1.9 copy-start.7
  100.4 1.0 copy-start.2
  100.9 1.8 copy-start.4
  131.6 14.5 %all-to-all-start.5 = ((bf16[8,128,128]{2,1,0:T(8,128)(2,1)}), bf16[8,128,128]{2,1,0:T(8,128)(2,1)}, u32[]{:S(2)}, u32[]{:S(2)}) async-start(bf16[8,128,128]{2,1,0:T(8,128)(2,1)} %bitcast.92), calls=%async_computation.6 | async-start | bytes 524288 | tf_op jit(solution)/shard_map/all_to_all | solution.py:156
  146.0 32.9 %all-to-all-start.4 = ((bf16[8,128,576]{1,2,0:T(8,128)(2,1)}), bf16[8,128,576]{1,2,0:T(8,128)(2,1)S(1)}, u32[]{:S(2)}, u32[]{:S(2)}) async-start(bf16[8,128,576]{1,2,0:T(8,128)(2,1)} %copy.30), calls=%async_computation.4 | async-start | bytes 2359296 | tf_op jit(solution)/shard_map/all_to_all | solution.py:155
  149.6 1.9 copy-start.6
  149.6 53.6 %all-gather.2.cloned.1.call-start = ((), (), s32[]{:S(2)}) async-start(), calls=%async_computation.8 | async-start | bytes 2621440 | tf_op jit(solution)/shard_map/all_gather | solution.py:188
  178.9 18.8 %all-to-all-start.2 = ((bf16[8,128,256]{1,2,0:T(8,128)(2,1)}), bf16[8,128,256]{1,2,0:T(8,128)(2,1)S(1)}, u32[]{:S(2)}, u32[]{:S(2)}) async-start(bf16[8,128,256]{1,2,0:T(8,128)(2,1)} %bitcast.69), calls=%async_computation.2 | async-start | bytes 1048576 | tf_op jit(solution)/shard_map/all_to_all | solution.py:154
  182.6 5.9 %collective-permute-start.4 = (bf16[128,4,24]{0,2,1:T(8,128)(2,1)S(1)}, bf16[128,4,24]{0,2,1:T(8,128)(2,1)S(1)}, u32[]{:S(2)}, u32[]{:S(2)}) collective-permute-start(bf16[128,4,24]{0,2,1:T(8,128)(2,1)S(1)} %get-tuple-element.96), channel_id=1, source_target_pairs={{16,0},{24,8},{17,1},{25,9},{18,2},{26,10},{19,3},{27,11},{20,4},{... | collective-permute-start | bytes 73736 | tf_op jit(solution)/shard_map/ppermute | solution.py:21
  184.0 6.1 %collective-permute-start.5 = (bf16[128,4,24]{0,2,1:T(8,128)(2,1)S(1)}, bf16[128,4,24]{0,2,1:T(8,128)(2,1)S(1)}, u32[]{:S(2)}, u32[]{:S(2)}) collective-permute-start(bf16[128,4,24]{0,2,1:T(8,128)(2,1)S(1)} %get-tuple-element.95), channel_id=1, source_target_pairs={{0,16},{8,24},{1,17},{9,25},{2,18},{10,26},{3,19},{11,27},{4,20},{... | collective-permute-start | bytes 73736 | tf_op jit(solution)/shard_map/ppermute | solution.py:21
  190.1 11.7 %collective-permute-start.6 = (bf16[128,16,4]{0,2,1:T(4,128)(2,1)S(1)}, bf16[128,16,4]{0,2,1:T(4,128)(2,1)S(1)}, u32[]{:S(2)}, u32[]{:S(2)}) collective-permute-start(bf16[128,16,4]{0,2,1:T(4,128)(2,1)S(1)} %get-tuple-element.98), channel_id=1, source_target_pairs={{8,0},{16,8},{24,16},{9,1},{17,9},{25,17},{10,2},{18,10},{26,18},{... | collective-permute-start | bytes 49160 | tf_op jit(solution)/shard_map/ppermute | solution.py:21
  198.4 4.8 %collective-permute-start.7 = (bf16[128,16,4]{0,2,1:T(4,128)(2,1)S(1)}, bf16[128,16,4]{0,2,1:T(4,128)(2,1)S(1)}, u32[]{:S(2)}, u32[]{:S(2)}) collective-permute-start(bf16[128,16,4]{0,2,1:T(4,128)(2,1)S(1)} %get-tuple-element.97), channel_id=1, source_target_pairs={{0,8},{8,16},{16,24},{1,9},{9,17},{17,25},{2,10},{10,18},{18,26},{... | collective-permute-start | bytes 49160 | tf_op jit(solution)/shard_map/ppermute | solution.py:21
  203.2 4.2 %copy-start.9 = (f32[1,128,16,16]{1,3,2,0:T(8,128)}, f32[1,128,16,16]{1,3,2,0:T(8,128)S(1)}, u32[]{:S(2)}) copy-start(f32[1,128,16,16]{1,3,2,0:T(8,128)S(1)} %fusion.27) | copy-start | bytes 393220
Sparse Core Ops, SparseCore 0:
  104.9 26.5 reduce-scatter.1
  152.5 35.9 all-gather.1
where the time goes:
time: 215 us; the launch traced here: 214 us
  waiting for transfers between devices  123 us (57%)
  starting transfers between devices  45.1 us (21%)
  local copies, waits for them, and re-layouts  19.2 us (9%)
  between operations  14.6 us (7%)
  matrix products  9.15 us (4%)
  other arithmetic  3.71 us (2%)
    all_to_all x1, waiting for transfers between devices, local(): lax.all_to_all(token_send, 'head', split_axis=0, concat_axis=1, tiled=True)  26.7 us
    reduce_scatter x1, waiting for transfers between devices, local(): lax.psum_scatter(spread.astype(jnp.bfloat16), 'tile', scatter_dimension=0...  25.3 us
    all_to_all x1, waiting for transfers between devices, local(): lax.all_to_all(grad_send_back, 'head', split_axis=0, concat_axis=0, tiled...  25.3 us
    ppermute x8, starting transfers between devices, passed_along(): lax.ppermute(value, axis, [(source, source + steps) for source in range(l...  19.9 us
    all_to_all x1, waiting for transfers between devices, local(): lax.all_to_all(grad_send, 'head', split_axis=0, concat_axis=1, tiled=True)  13.6 us
    ppermute x8, waiting for transfers between devices, passed_along(): lax.ppermute(value, axis, [(source, source + steps) for source in range(l...  11.6 us
    all_to_all x1, waiting for transfers between devices, local(): lax.all_to_all(weight_send, 'head', split_axis=0, concat_axis=1, tiled=True)  8.15 us
    dot_general x11, matrix products, contract(): lax.dot_general(first_op, second_op, (((first_dim,), (second_dim,)), ((),...  7.65 us
  transfers between devices with their start and end apart: 16, of which 13 were waited for; matrix products, arithmetic and copies ran while one was open for 7% of the time, Pallas kernels for 0%

commit v1 on v0

--- a/solution.py
+++ b/solution.py
@@ -1,6 +1,8 @@
 import jax
 import jax.numpy as jnp
 from jax import lax
+from jax.experimental import pallas as pl
+from jax.experimental.pallas import tpu as pltpu
 from jax.sharding import PartitionSpec as P
 
 D = 1024
@@ -192,14 +194,346 @@
     return (attention, token_grads, weight_grads)
 
 
+BF16 = jnp.bfloat16
+F32 = jnp.float32
+MESH = pl.DeviceIdType.MESH
+SIDE = TILE_ROWS * RIM
+FLAT = TILE_COLS * RIM
+CORNER = RIM * RIM
+RIM_TOKENS = SIDE + FLAT + CORNER
+REACH = TILE_TOKENS + RIM_TOKENS
+KEY_SLOTS = -(-REACH // 128) * 128
+
+
+def flip(value, by):
+    low, high = by % 2, by // 2
+    value_low, value_high = value % 2, value // 2
+    value_low = value_low + low - 2 * low * value_low
+    value_high = value_high + high - 2 * high * value_high
+    return value_low + 2 * value_high
+
+
+def block(index, size=HEAD_DIM):
+    return pl.ds(pl.multiple_of(index * size, size), size)
+
+
+def rim_choice(tile_id):
+    first_row = (TILE_ROWS - RIM) * (1 - tile_id // 2)
+    first_col = (TILE_COLS - RIM) * (1 - tile_id % 2)
+    row = lax.broadcasted_iota(jnp.int32, (RIM_TOKENS, TILE_TOKENS), 0)
+    token = lax.broadcasted_iota(jnp.int32, (RIM_TOKENS, TILE_TOKENS), 1)
+    token_row = lax.div(token, jnp.int32(TILE_COLS))
+    token_col = lax.rem(token, jnp.int32(TILE_COLS))
+    beside = (
+        (token_row == lax.div(row, jnp.int32(RIM)))
+        & (token_col == first_col + lax.rem(row, jnp.int32(RIM)))
+        & (row < SIDE)
+    )
+    flat = row - SIDE
+    above = (token == first_row * TILE_COLS + flat) & (flat >= 0) & (flat < FLAT)
+    corner = jnp.maximum(row - SIDE - FLAT, 0)
+    across = (
+        (token_row == first_row + lax.div(corner, jnp.int32(RIM)))
+        & (token_col == first_col + lax.rem(corner, jnp.int32(RIM)))
+        & (row >= SIDE + FLAT)
+    )
+    return jnp.where(beside | above | across, 1.0, 0.0).astype(BF16)
+
+
+RIM_SPANS = (
+    pl.ds(0, SIDE),
+    pl.ds(SIDE, FLAT),
+    pl.ds(SIDE + FLAT, CORNER),
+)
+KEY_SPANS = (
+    pl.ds(TILE_TOKENS, SIDE),
+    pl.ds(TILE_TOKENS + SIDE, FLAT),
+    pl.ds(TILE_TOKENS + SIDE + FLAT, CORNER),
+)
+
+
+def fused_kernel(
+    xg_ref, w_ref, att_ref, dx_ref, dw_ref,
+    xg_all, w_all, kv_send, kv_all, dkv, ret, heads_all, part, got,
+    xg_ss, xg_rs, wz_ss, wz_rs, wt_ss, wt_rs, kv_ss, kv_rs, ret_ss, ret_rs,
+    hg_ss, hg_rs, rs_ss, rs_rs, ag_ss, ag_rs,
+):
+    tile_id = lax.axis_index("tile")
+    head_id = lax.axis_index("head")
+    chip, core = head_id // 2, head_id % 2
+    n_tile = 4
+    n_chip = HEADS // 2
+    share = HEADS * HEAD_DIM // n_tile
+    score_scale = HEAD_DIM ** (-0.5)
+
+    def copy(src, dst, send_sem, recv_sem, tile, head):
+        return pltpu.make_async_remote_copy(
+            src_ref=src, dst_ref=dst, send_sem=send_sem, recv_sem=recv_sem,
+            device_id={"tile": tile, "head": head}, device_id_type=MESH,
+        )
+
+    def holder(by):
+        return 2 * flip(chip, by // 2) + (core + (by % 2) - 2 * (by % 2) * core)
+
+    barrier = pltpu.get_barrier_semaphore()
+    for by in range(1, HEADS):
+        pl.semaphore_signal(
+            barrier, inc=1, device_id={"tile": tile_id, "head": holder(by)}, device_id_type=MESH
+        )
+    for by in range(1, n_tile):
+        pl.semaphore_signal(
+            barrier, inc=1, device_id={"tile": flip(tile_id, by), "head": head_id},
+            device_id_type=MESH,
+        )
+    pl.semaphore_wait(barrier, HEADS + n_tile - 2)
+
+    sent = []
+
+    def go(one):
+        one.start()
+        sent.append(one)
+        return one
+
+    class Gather:
+        def __init__(self, src, view, ss, rs):
+            self.src, self.view, self.ss, self.rs = src, view, ss, rs
+
+        def start(self):
+            for by in list(range(2, HEADS, 2)) + [1]:
+                self.start_one(by)
+
+        def start_one(self, by):
+            go(copy(self.src, self.view(head_id), self.ss.at[by], self.rs.at[by], tile_id, holder(by)))
+
+        def wait(self, by):
+            view = self.view(holder(by))
+            copy(view, view, self.ss.at[by], self.rs.at[by], tile_id, head_id).wait_recv()
+
+        def pass_on(self, by):
+            self.wait(by)
+            view = self.view(holder(by))
+            go(copy(view, view, self.ss.at[by + 1], self.rs.at[by + 1], tile_id, holder(1)))
+
+        def finish(self):
+            for by in range(1, HEADS, 2):
+                self.wait(by)
+
+    gathers = [
+        Gather(
+            xg_ref.at[n],
+            lambda holder_id, n=n: xg_all.at[n, :, block(holder_id)],
+            xg_ss.at[n], xg_rs.at[n],
+        )
+        for n in range(2)
+    ]
+    gathers[0].start()
+    for by in range(1, HEADS):
+        to = holder(by)
+        go(
+            copy(
+                w_ref.at[tile_id, :, block(to)],
+                w_all.at[block(head_id), block(tile_id)],
+                wz_ss.at[by], wz_rs.at[by], tile_id, to,
+            )
+        )
+    gathers[1].start()
+    for n in range(2):
+        xg_all[n, :, block(head_id)] = xg_ref[n]
+    w_all[block(head_id), block(tile_id)] = w_ref[tile_id, :, block(head_id)]
+    kv_all[REACH:] = jnp.zeros((KEY_SLOTS - REACH, 2 * HEAD_DIM), BF16)
+    choice = rim_choice(tile_id)
+    x_rows = xg_ref[0].astype(F32).T.astype(BF16)
+    g_rows = xg_ref[1].astype(F32).T.astype(BF16)
+
+    two = 2 * HEAD_DIM
+    for by_chip in range(n_chip):
+        if by_chip > 0:
+            gathers[0].pass_on(2 * by_chip)
+        for by in (2 * by_chip, 2 * by_chip + 1):
+            if by > 0:
+                view = w_all.at[block(holder(by)), block(tile_id)]
+                copy(view, view, wz_ss.at[by], wz_rs.at[by], tile_id, head_id).wait_recv()
+        view = w_all.at[block(flip(chip, by_chip), two), block(tile_id)]
+        for by in range(1, n_tile):
+            slot = by_chip * n_tile + by
+            go(copy(view, view, wt_ss.at[slot], wt_rs.at[slot], flip(tile_id, by), head_id))
+    for by_chip in range(1, n_chip):
+        gathers[1].pass_on(2 * by_chip)
+    gathers[0].finish()
+    for by_chip in range(n_chip):
+        for by in range(1, n_tile):
+            slot = by_chip * n_tile + by
+            view = w_all.at[block(flip(chip, by_chip), two), block(flip(tile_id, by))]
+            copy(view, view, wt_ss.at[slot], wt_rs.at[slot], tile_id, head_id).wait_recv()
+
+    qkv = jnp.dot(xg_all[0], w_all[:, : 3 * HEAD_DIM], preferred_element_type=F32).astype(BF16)
+    queries = qkv[:, :HEAD_DIM]
+    own_kv = qkv[:, HEAD_DIM:]
+    kv_send[...] = jnp.dot(choice, own_kv, preferred_element_type=F32).astype(BF16)
+    for by in range(1, n_tile):
+        go(
+            copy(
+                kv_send.at[RIM_SPANS[by - 1]], kv_all.at[KEY_SPANS[by - 1]],
+                kv_ss.at[by], kv_rs.at[by], flip(tile_id, by), head_id,
+            )
+        )
+    gathers[1].finish()
+    d_attended = jnp.dot(
+        xg_all[1], w_all[:, 3 * HEAD_DIM :], preferred_element_type=F32
+    ).astype(BF16)
+    for by in range(1, n_tile):
+        view = kv_all.at[KEY_SPANS[by - 1]]
+        copy(view, view, kv_ss.at[by], kv_rs.at[by], tile_id, head_id).wait_recv()
+    rim_kv = kv_all[TILE_TOKENS:]
+    keys = jnp.concatenate([own_kv[:, :HEAD_DIM], rim_kv[:, :HEAD_DIM]], 0)
+    values = jnp.concatenate([own_kv[:, HEAD_DIM:], rim_kv[:, HEAD_DIM:]], 0)
+
+    scores = contract(queries, keys, 1, 1) * score_scale
+    slot_id = lax.broadcasted_iota(jnp.int32, scores.shape, 1)
+    scores = jnp.where(slot_id < REACH, scores, -jnp.inf)
+    top_score = jnp.max(scores, axis=-1, keepdims=True)
+    expo = jnp.exp(scores - top_score)
+    probs = expo / jnp.sum(expo, axis=-1, keepdims=True)
+    probs_low = probs.astype(BF16)
+
+    head_gathers = [
+        Gather(
+            heads_all.at[m, :, block(head_id)],
+            lambda holder_id, m=m: heads_all.at[m, :, block(holder_id)],
+            hg_ss.at[m], hg_rs.at[m],
+        )
+        for m in range(4)
+    ]
+    attended = jnp.dot(probs_low, values, preferred_element_type=F32).astype(BF16)
+    heads_all[3, :, block(head_id)] = attended
+    head_gathers[3].start()
+    d_values = contract(probs_low, d_attended, 0, 0)
+    d_probs = contract(d_attended, values, 1, 1)
+    d_scores = (
+        probs * (d_probs - jnp.sum(d_probs * probs, axis=-1, keepdims=True)) * score_scale
+    ).astype(BF16)
+    d_keys = contract(d_scores, queries, 0, 0)
+    d_keyval = jnp.concatenate([d_keys, d_values], 1)
+    dkv[...] = d_keyval[TILE_TOKENS:].astype(BF16)
+    for by in range(1, n_tile):
+        span = RIM_SPANS[by - 1]
+        go(copy(dkv.at[span], ret.at[span], ret_ss.at[by], ret_rs.at[by], flip(tile_id, by), head_id))
+    heads_all[0, :, block(head_id)] = jnp.dot(
+        d_scores, keys, preferred_element_type=F32
+    ).astype(BF16)
+    head_gathers[0].start()
+    for by in range(1, n_tile):
+        view = ret.at[RIM_SPANS[by - 1]]
+        copy(view, view, ret_ss.at[by], ret_rs.at[by], tile_id, head_id).wait_recv()
+    d_keyval = (d_keyval[:TILE_TOKENS] + contract(choice, ret[...], 0, 0)).astype(BF16)
+    heads_all[1, :, block(head_id)] = d_keyval[:, :HEAD_DIM]
+    heads_all[2, :, block(head_id)] = d_keyval[:, HEAD_DIM:]
+    head_gathers[1].start()
+    head_gathers[2].start()
+
+    def sum_out(m):
+        for by in range(1, n_tile):
+            view = got.at[m, by - 1]
+            copy(view, view, rs_ss.at[m, by], rs_rs.at[m, by], tile_id, head_id).wait_recv()
+        total = part[m, :, block(tile_id, share)].astype(F32)
+        for by in range(1, n_tile):
+            total = total + got[m, by - 1].astype(F32)
+        dw_ref[m, :, block(tile_id, share)] = total.astype(BF16)
+        view = dw_ref.at[m, :, block(tile_id, share)]
+        for by in range(1, n_tile):
+            go(copy(view, view, ag_ss.at[m, by], ag_rs.at[m, by], flip(tile_id, by), head_id))
+
+    d_tokens = None
+    order = (3, 0, 1, 2)
+    for place, m in enumerate(order):
+        for by_chip in range(1, n_chip):
+            head_gathers[m].pass_on(2 * by_chip)
+        head_gathers[m].finish()
+        all_heads = heads_all[m]
+        rows = g_rows if m == 3 else x_rows
+        part[m] = jnp.dot(rows, all_heads, preferred_element_type=F32).astype(BF16)
+        for by in range(1, n_tile):
+            to = flip(tile_id, by)
+            go(
+                copy(
+                    part.at[m, :, block(to, share)], got.at[m, by - 1],
+                    rs_ss.at[m, by], rs_rs.at[m, by], to, head_id,
+                )
+            )
+        back = contract(w_ref[m], all_heads, 1, 1)
+        if m == 3:
+            att_ref[...] = back.astype(BF16)
+        else:
+            d_tokens = back if d_tokens is None else d_tokens + back
+        if place > 0:
+            sum_out(order[place - 1])
+    dx_ref[...] = d_tokens
+    sum_out(order[-1])
+    for m in order:
+        for by in range(1, n_tile):
+            view = dw_ref.at[m, :, block(flip(tile_id, by), share)]
+            copy(view, view, ag_ss.at[m, by], ag_rs.at[m, by], tile_id, head_id).wait_recv()
+    for one in sent:
+        one.wait_send()
+
+
+def local_fused(embedded, cotangent, weights):
+    n_tile = lax.axis_size("tile")
+    width_part = embedded.shape[1]
+    tokens = jnp.concatenate([embedded, cotangent], 0).reshape(2, width_part, TILE_TOKENS)
+    tokens = tokens.transpose(0, 2, 1)
+    flat_weights = weights.transpose(1, 0, 2, 3).reshape(4, width_part, HEADS * HEAD_DIM)
+    vmem = pl.BlockSpec(memory_space=pltpu.VMEM)
+    dma = pltpu.SemaphoreType.DMA
+    whole = HEADS * HEAD_DIM
+    attention, token_grads, weight_grads = pl.pallas_call(
+        fused_kernel,
+        out_shape=(
+            jax.ShapeDtypeStruct((width_part, TILE_TOKENS), BF16),
+            jax.ShapeDtypeStruct((width_part, TILE_TOKENS), F32),
+            jax.ShapeDtypeStruct((4, width_part, whole), BF16),
+        ),
+        in_specs=[vmem] * 2,
+        out_specs=(vmem,) * 3,
+        scratch_shapes=[
+            pltpu.VMEM((2, TILE_TOKENS, D), BF16),
+            pltpu.VMEM((D, 4 * HEAD_DIM), BF16),
+            pltpu.VMEM((RIM_TOKENS, 2 * HEAD_DIM), BF16),
+            pltpu.VMEM((KEY_SLOTS, 2 * HEAD_DIM), BF16),
+            pltpu.VMEM((KEY_SLOTS - TILE_TOKENS, 2 * HEAD_DIM), BF16),
+            pltpu.VMEM((RIM_TOKENS, 2 * HEAD_DIM), BF16),
+            pltpu.VMEM((4, TILE_TOKENS, whole), BF16),
+            pltpu.VMEM((4, width_part, whole), BF16),
+            pltpu.VMEM((4, n_tile - 1, width_part, whole // n_tile), BF16),
+            dma((2, HEADS)), dma((2, HEADS)),
+            dma((HEADS,)), dma((HEADS,)),
+            dma((HEADS // 2 * n_tile,)), dma((HEADS // 2 * n_tile,)),
+            dma((n_tile,)), dma((n_tile,)),
+            dma((n_tile,)), dma((n_tile,)),
+            dma((4, HEADS)), dma((4, HEADS)),
+            dma((4, n_tile)), dma((4, n_tile)),
+            dma((4, n_tile)), dma((4, n_tile)),
+        ],
+        compiler_params=pltpu.CompilerParams(
+            collective_id=0, has_side_effects=True, vmem_limit_bytes=48 * 2**20
+        ),
+    )(tokens, flat_weights)
+    return (
+        attention.reshape(embedded.shape),
+        token_grads.reshape(embedded.shape),
+        weight_grads.astype(F32).reshape(4, width_part, HEADS, HEAD_DIM).transpose(1, 0, 2, 3),
+    )
+
+
 def solution(mesh):
+    one_tile_each = mesh.shape["head"] == HEADS and mesh.shape["tile"] == 2 * 2
     placed = (
         P("tile", "head", None, None),
         P("tile", "head", None, None),
         P("head", None, None, None),
     )
     return jax.shard_map(
-        local,
+        local_fused if one_tile_each else local,
         mesh=mesh,
         in_specs=placed,
         out_specs=(

time: 215 us -> 80.4 us (0.37)
  waiting for transfers between devices: 123 us -> 0 us
  Pallas kernels: 0 us -> 72.5 us
  starting transfers between devices: 45.1 us -> 0 us
  local copies, waits for them, and re-layouts: 19.2 us -> 5.02 us
  between operations: 14.6 us -> 0.67 us
  matrix products: 9.15 us -> 0 us
  other arithmetic: 3.71 us -> 0.89 us
    all_to_all x6 -> x0, waiting for transfers between devices: 85.6 us -> none  [the longest x1 26.7 us: local(): lax.all_to_all(token_send, 'head', split_axis=0, concat_axis=1, tiled=True)]
    pallas_call x0 -> x1, Pallas kernels: none -> 72.5 us  [local_fused(): pl.pallas_call(fused_kernel, out_shape=(jax.ShapeDtypeStruct((width_part,...]
    reduce_scatter x1 -> x0, waiting for transfers between devices: 25.3 us -> none  [local(): lax.psum_scatter(spread.astype(jnp.bfloat16), 'tile', scatter_dimension=0...]
    all_to_all x6 -> x0, starting transfers between devices: 25.1 us -> none  [the longest x1 6.33 us: local(): lax.all_to_all(grad_send, 'head', split_axis=0, concat_axis=1, tiled=True)]
    ppermute x8 -> x0, starting transfers between devices: 19.9 us -> none  [passed_along(): lax.ppermute(value, axis, [(source, source + steps) for source in range(l...]
    ppermute x8 -> x0, waiting for transfers between devices: 11.6 us -> none  [passed_along(): lax.ppermute(value, axis, [(source, source + steps) for source in range(l...]
    dot_general x15 -> x0, matrix products: 9.15 us -> none  [the longest x11 7.65 us: contract(): lax.dot_general(first_op, second_op, (((first_dim,), (second_dim,)), ((),...]
    unnamed x24 -> x1, local copies, waits for them, and re-layouts: 6.54 us -> 0.26 us
  transfers between devices with their start and end apart: 16 -> 0, of which waited for: 13 -> 0; matrix products, arithmetic and copies ran while one was open for 7% -> 0% of each run, Pallas kernels for 0% -> 0%
where the time goes in v1:
time: 80.4 us; the launch traced here: 79.1 us
  Pallas kernels  72.5 us (90%)
  local copies, waits for them, and re-layouts  5.02 us (6%)
  other arithmetic  0.89 us (1%)
    pallas_call x1, Pallas kernels, local_fused(): pl.pallas_call(fused_kernel, out_shape=(jax.ShapeDtypeStruct((width_part,...  72.5 us
    reshape x2, local copies, waits for them, and re-layouts, local_fused(): weights.transpose(1, 0, 2, 3).reshape(4, width_part, HEADS * HEAD_DIM)  1.66 us
    transpose x1, local copies, waits for them, and re-layouts, local_fused(): weight_grads.astype(F32).reshape(4, width_part, HEADS, HEAD_DIM)  1.62 us

profile of v1, /device:TPU:0, one launch (start us, length us, event | category | flops | bytes accessed | tf_op | source)
XLA Modules:
  0.0 79.1 jit_solution(2653619873281904950)
XLA Ops:
  0.6 0.9 %pad_maximum_fusion = bf16[2,128,16,16]{1,3,2,0:T(8,128)(2,1)S(1)} fusion(bf16[1,128,16,16]{1,3,2,0:T(8,128)(2,1)} %param.4, bf16[1,128,16,16]{1,3,2,0:T(8,128)(2,1)} %param.3), kind=kLoop, calls=%fused_computation.1 | loop fusion | flops 65536 | bytes 262144 | tf_op jit(solution)/shard_map/concatenate | solution.py:483
  1.5 1.3 %reshape.28 = bf16[4,128,1024]{2,0,1:T(4,128)(2,1)S(1)} reshape(bf16[4,128,8,128]{3,2,0,1:T(8,128)(2,1)} %bitcast.24) | data formatting | bytes 2097152 | tf_op jit(solution)/shard_map/reshape | solution.py:485
  2.9 0.3 copy.14.w_ref
  3.2 72.5 %shard_map.58 = (bf16[128,256]{1,0:T(8,128)(2,1)S(1)}, f32[128,256]{1,0:T(8,128)S(1)}, bf16[4,128,1024]{2,1,0:T(8,128)(2,1)S(1)}) custom-call(bf16[2,256,128]{2,1,0:T(8,128)(2,1)S(1)} %bitcast.22, bf16[4,128,1024]{2,1,0:T(8,128)(2,1)S(1)} %copy.14.w_ref), custom_call_target="tpu_custom_call" | custom-call | tf_op jit(solution)/shard_map/pallas_call | solution.py:489
  75.7 0.7 copy.11
  76.5 0.8 copy.12
  77.2 0.3 copy.15
  77.5 1.6 %copy_bitcast_fusion = f32[128,4,8,128]{3,2,1,0:T(8,128)} fusion(f32[4,128,8,128]{3,2,1,0:T(8,128)S(1)} %bitcast.23), kind=kLoop, calls=%fused_computation | loop fusion | bytes 4194304 | tf_op jit(solution)/shard_map/transpose | solution.py:524

commit v2 on v1

--- a/solution.py
+++ b/solution.py
@@ -336,7 +336,6 @@
                 wz_ss.at[by], wz_rs.at[by], tile_id, to,
             )
         )
-    gathers[1].start()
     for n in range(2):
         xg_all[n, :, block(head_id)] = xg_ref[n]
     w_all[block(head_id), block(tile_id)] = w_ref[tile_id, :, block(head_id)]
@@ -357,8 +356,7 @@
         for by in range(1, n_tile):
             slot = by_chip * n_tile + by
             go(copy(view, view, wt_ss.at[slot], wt_rs.at[slot], flip(tile_id, by), head_id))
-    for by_chip in range(1, n_chip):
-        gathers[1].pass_on(2 * by_chip)
+    gathers[1].start()
     gathers[0].finish()
     for by_chip in range(n_chip):
         for by in range(1, n_tile):
@@ -377,10 +375,8 @@
                 kv_ss.at[by], kv_rs.at[by], flip(tile_id, by), head_id,
             )
         )
-    gathers[1].finish()
-    d_attended = jnp.dot(
-        xg_all[1], w_all[:, 3 * HEAD_DIM :], preferred_element_type=F32
-    ).astype(BF16)
+    for by_chip in range(1, n_chip):
+        gathers[1].pass_on(2 * by_chip)
     for by in range(1, n_tile):
         view = kv_all.at[KEY_SPANS[by - 1]]
         copy(view, view, kv_ss.at[by], kv_rs.at[by], tile_id, head_id).wait_recv()
@@ -407,6 +403,10 @@
     attended = jnp.dot(probs_low, values, preferred_element_type=F32).astype(BF16)
     heads_all[3, :, block(head_id)] = attended
     head_gathers[3].start()
+    gathers[1].finish()
+    d_attended = jnp.dot(
+        xg_all[1], w_all[:, 3 * HEAD_DIM :], preferred_element_type=F32
+    ).astype(BF16)
     d_values = contract(probs_low, d_attended, 0, 0)
     d_probs = contract(d_attended, values, 1, 1)
     d_scores = (
@@ -428,8 +428,6 @@
     d_keyval = (d_keyval[:TILE_TOKENS] + contract(choice, ret[...], 0, 0)).astype(BF16)
     heads_all[1, :, block(head_id)] = d_keyval[:, :HEAD_DIM]
     heads_all[2, :, block(head_id)] = d_keyval[:, HEAD_DIM:]
-    head_gathers[1].start()
-    head_gathers[2].start()
 
     def sum_out(m):
         for by in range(1, n_tile):
@@ -448,6 +446,8 @@
     for place, m in enumerate(order):
         for by_chip in range(1, n_chip):
             head_gathers[m].pass_on(2 * by_chip)
+        if place + 2 < len(order):
+            head_gathers[order[place + 2]].start()
         head_gathers[m].finish()
         all_heads = heads_all[m]
         rows = g_rows if m == 3 else x_rows

time: 80.4 us -> 78.5 us (0.976)
  the two profiles are of different devices: /device:TPU:0 before, /device:TPU:9 now
where the time goes in v2:
time: 78.5 us; the launch traced here: 78.3 us
  Pallas kernels  71.7 us (91%)
  local copies, waits for them, and re-layouts  5.02 us (6%)
  other arithmetic  0.89 us (1%)
    pallas_call x1, Pallas kernels, local_fused(): pl.pallas_call(fused_kernel, out_shape=(jax.ShapeDtypeStruct((width_part,...  71.7 us
    reshape x2, local copies, waits for them, and re-layouts, local_fused(): weights.transpose(1, 0, 2, 3).reshape(4, width_part, HEADS * HEAD_DIM)  1.66 us
    transpose x1, local copies, waits for them, and re-layouts, local_fused(): weight_grads.astype(F32).reshape(4, width_part, HEADS, HEAD_DIM)  1.62 us

profile of v2, /device:TPU:9, one launch (start us, length us, event | category | flops | bytes accessed | tf_op | source)
XLA Modules:
  0.0 78.3 jit_solution(15996503756644231051)
XLA Ops:
  0.6 0.9 %pad_maximum_fusion = bf16[2,128,16,16]{1,3,2,0:T(8,128)(2,1)S(1)} fusion(bf16[1,128,16,16]{1,3,2,0:T(8,128)(2,1)} %param.4, bf16[1,128,16,16]{1,3,2,0:T(8,128)(2,1)} %param.3), kind=kLoop, calls=%fused_computation.1 | loop fusion | flops 65536 | bytes 262144 | tf_op jit(solution)/shard_map/concatenate | solution.py:483
  1.5 1.3 %reshape.28 = bf16[4,128,1024]{2,0,1:T(4,128)(2,1)S(1)} reshape(bf16[4,128,8,128]{3,2,0,1:T(8,128)(2,1)} %bitcast.24) | data formatting | bytes 2097152 | tf_op jit(solution)/shard_map/reshape | solution.py:485
  2.9 0.3 copy.14.w_ref
  3.2 71.7 %shard_map.58 = (bf16[128,256]{1,0:T(8,128)(2,1)S(1)}, f32[128,256]{1,0:T(8,128)S(1)}, bf16[4,128,1024]{2,1,0:T(8,128)(2,1)S(1)}) custom-call(bf16[2,256,128]{2,1,0:T(8,128)(2,1)S(1)} %bitcast.22, bf16[4,128,1024]{2,1,0:T(8,128)(2,1)S(1)} %copy.14.w_ref), custom_call_target="tpu_custom_call" | custom-call | tf_op jit(solution)/shard_map/pallas_call | solution.py:489
  74.9 0.7 copy.11
  75.6 0.8 copy.12
  76.4 0.3 copy.15
  76.7 1.6 %copy_bitcast_fusion = f32[128,4,8,128]{3,2,1,0:T(8,128)} fusion(f32[4,128,8,128]{3,2,1,0:T(8,128)S(1)} %bitcast.23), kind=kLoop, calls=%fused_computation | loop fusion | bytes 4194304 | tf_op jit(solution)/shard_map/transpose | solution.py:524

commit v3 on v2

--- a/solution.py
+++ b/solution.py
@@ -446,6 +446,8 @@
     for place, m in enumerate(order):
         for by_chip in range(1, n_chip):
             head_gathers[m].pass_on(2 * by_chip)
+            if place > 0 and by_chip == 2:
+                sum_out(order[place - 1])
         if place + 2 < len(order):
             head_gathers[order[place + 2]].start()
         head_gathers[m].finish()
@@ -465,8 +467,6 @@
             att_ref[...] = back.astype(BF16)
         else:
             d_tokens = back if d_tokens is None else d_tokens + back
-        if place > 0:
-            sum_out(order[place - 1])
     dx_ref[...] = d_tokens
     sum_out(order[-1])
     for m in order:

time: 78.5 us -> 81.2 us (1.034)
  the two profiles are of different devices: /device:TPU:9 before, /device:TPU:0 now
where the time goes in v3:
time: 81.2 us; the launch traced here: 81 us
  Pallas kernels  74.4 us (92%)
  local copies, waits for them, and re-layouts  5.02 us (6%)
  other arithmetic  0.89 us (1%)
    pallas_call x1, Pallas kernels, local_fused(): pl.pallas_call(fused_kernel, out_shape=(jax.ShapeDtypeStruct((width_part,...  74.4 us
    reshape x2, local copies, waits for them, and re-layouts, local_fused(): weights.transpose(1, 0, 2, 3).reshape(4, width_part, HEADS * HEAD_DIM)  1.66 us

profile of v3, /device:TPU:0, one launch (start us, length us, event | category | flops | bytes accessed | tf_op | source)
XLA Modules:
  0.0 81.0 jit_solution(16609087394768157745)
XLA Ops:
  0.6 0.9 %pad_maximum_fusion = bf16[2,128,16,16]{1,3,2,0:T(8,128)(2,1)S(1)} fusion(bf16[1,128,16,16]{1,3,2,0:T(8,128)(2,1)} %param.4, bf16[1,128,16,16]{1,3,2,0:T(8,128)(2,1)} %param.3), kind=kLoop, calls=%fused_computation.1 | loop fusion | flops 65536 | bytes 262144 | tf_op jit(solution)/shard_map/concatenate | solution.py:483
  1.5 1.3 %reshape.28 = bf16[4,128,1024]{2,0,1:T(4,128)(2,1)S(1)} reshape(bf16[4,128,8,128]{3,2,0,1:T(8,128)(2,1)} %bitcast.24) | data formatting | bytes 2097152 | tf_op jit(solution)/shard_map/reshape | solution.py:485
  2.9 0.3 copy.14.w_ref
  3.2 74.4 %shard_map.58 = (bf16[128,256]{1,0:T(8,128)(2,1)S(1)}, f32[128,256]{1,0:T(8,128)S(1)}, bf16[4,128,1024]{2,1,0:T(8,128)(2,1)S(1)}) custom-call(bf16[2,256,128]{2,1,0:T(8,128)(2,1)S(1)} %bitcast.22, bf16[4,128,1024]{2,1,0:T(8,128)(2,1)S(1)} %copy.14.w_ref), custom_call_target="tpu_custom_call" | custom-call | tf_op jit(solution)/shard_map/pallas_call | solution.py:489
  77.6 0.7 copy.11
  78.3 0.8 copy.12
  79.1 0.3 copy.15
  79.4 1.6 %copy_bitcast_fusion = f32[128,4,8,128]{3,2,1,0:T(8,128)} fusion(f32[4,128,8,128]{3,2,1,0:T(8,128)S(1)} %bitcast.23), kind=kLoop, calls=%fused_computation | loop fusion | bytes 4194304 | tf_op jit(solution)/shard_map/transpose | solution.py:524
